TPU v7x, 32 devices: a whole 2x2x4 slice. The times are simulated.
32 devices in a mesh: seq: 16 (over z, y, x), head: 2 (over core).
Axes of the slice: x: 2, y: 2, z: 4, core: 2. Of those that a mesh axis runs over, the one named last changes fastest.
Arguments:
- layer_input: bfloat16 [8192, 5376], P('seq', 'head'), may hold values from -6 to 6
- omega_in: bfloat16 [5376, 128], P('head'), may hold values from -0.0078125 to 0.0078125
- upstream: bfloat16 [8192, 5376], P('seq', 'head'), may hold values from -6 to 6
- omega_out: bfloat16 [5376, 128], P('head'), may hold values from -0.0078125 to 0.0078125
- q_raw: bfloat16 [8192, 4096], P('seq', 'head'), may hold values from -6 to 6
- k_raw: bfloat16 [8192, 2048], P('seq', 'head'), may hold values from -6 to 6
- values: bfloat16 [8192, 2048], P('seq', 'head'), may hold values from -6 to 6
- d_out: bfloat16 [8192, 4096], P('seq', 'head'), may hold values from -16 to 16
- q_gain: float32 [128], replicated, may hold values from 0.1 to 1.9
- k_gain: float32 [128], replicated, may hold values from 0.1 to 1.9
Outputs:
- query_grad: bfloat16 [8192, 4096], P('seq', 'head')
- key_grad: bfloat16 [8192, 2048], P('seq', 'head')
- value_grad: bfloat16 [8192, 2048], P('seq', 'head')
- sketch_q: float32 [128, 4096], P('seq', 'head')
- sketch_k: float32 [128, 2048], P('seq', 'head')
- sketch_v: float32 [128, 2048], P('seq', 'head')
- sketch_o: float32 [128, 4096], P('seq', 'head')
All inputs are finite; a program needn't handle non-finite values.
Results may differ from a plain program's by a relative error of at most 0.013.
Values may be sent and summed in bfloat16 or wider, within the bound.
A program may use at most 128 MiB of HBM per device.

v0:
```python
import jax
import jax.numpy as jnp
from jax import lax
from jax.sharding import PartitionSpec as P

WINDOW = 1024


score_scale = 168.0 ** (-0.5)
epsilon = 1e-06
rope_base = 10000.0


def from_behind(shard, axis, by):
    count = lax.axis_size(axis)
    pairs = [(i, i + by) for i in range(count) if 0 <= i + by < count]
    return lax.ppermute(shard, axis, pairs)


def prepare(raw_input, gain, positions):
    mean_square = jnp.mean(raw_input * raw_input, axis=-1, keepdims=True)
    normed = raw_input * lax.rsqrt(mean_square + epsilon) * gain
    half_dim = raw_input.shape[-1] // 2
    inverse_freq = rope_base ** (
        -(jnp.arange(half_dim, dtype=jnp.float32) * 2.0 / raw_input.shape[-1])
    )
    angles = positions.astype(jnp.float32)[:, None] * inverse_freq[None, :]
    cos_table = jnp.cos(angles)[:, None, :]
    sin_table = jnp.sin(angles)[:, None, :]
    lower_half = normed[..., :half_dim]
    upper_half = normed[..., half_dim:]
    return jnp.concatenate(
        [
            lower_half * cos_table - upper_half * sin_table,
            upper_half * cos_table + lower_half * sin_table,
        ],
        axis=-1,
    )


def head_core(query_rows, key_rows, value_rows, grad_rows, allowed):
    scores = score_scale * jnp.dot(query_rows, key_rows.T, preferred_element_type=jnp.float32)
    exp_scores = jnp.where(allowed, jnp.exp(scores), 0.0)
    probs = exp_scores / jnp.sum(exp_scores, axis=-1, keepdims=True)
    probs_low = probs.astype(jnp.bfloat16)
    attn_rows = jnp.dot(probs_low, value_rows, preferred_element_type=jnp.float32).astype(
        jnp.bfloat16
    )
    grad_probs = jnp.dot(grad_rows, value_rows.T, preferred_element_type=jnp.float32)
    row_delta = jnp.sum(probs * grad_probs, axis=-1, keepdims=True)
    grad_low = (probs * (grad_probs - row_delta)).astype(jnp.bfloat16)
    query_grad = score_scale * jnp.dot(grad_low, key_rows, preferred_element_type=jnp.float32)
    key_grad = score_scale * jnp.dot(grad_low.T, query_rows, preferred_element_type=jnp.float32)
    value_grad = jnp.dot(probs_low.T, grad_rows, preferred_element_type=jnp.float32)
    return (attn_rows, query_grad, key_grad, value_grad)


def per_device(
    layer_input, omega_in, upstream, omega_out, q_raw, k_raw, values, d_out, q_gain, k_gain
):
    tok_rows = q_raw.shape[0]
    head_dim = q_gain.shape[0]
    heads_q = q_raw.shape[1] // head_dim
    heads_kv = k_raw.shape[1] // head_dim
    group_size = heads_q // heads_kv
    kv_cols = heads_kv * head_dim
    q_cols = heads_q * head_dim
    halo_devices = (WINDOW + tok_rows - 1) // tok_rows
    ext_rows = halo_devices * tok_rows
    span_rows = ext_rows + tok_rows
    partial_x = jnp.dot(layer_input, omega_in, preferred_element_type=jnp.float32)
    partial_y = jnp.dot(upstream, omega_out, preferred_element_type=jnp.float32)
    summed_x, summed_y = lax.psum((partial_x, partial_y), "head")
    x_sketch = summed_x.astype(jnp.bfloat16)
    dy_sketch = summed_y.astype(jnp.bfloat16)
    offset = lax.axis_index("seq") * tok_rows
    positions = offset + jnp.arange(tok_rows, dtype=jnp.int32)
    query_f = q_raw.astype(jnp.float32).reshape(tok_rows, heads_q, head_dim)
    key_f = k_raw.astype(jnp.float32).reshape(tok_rows, heads_kv, head_dim)
    query_full, query_back = jax.vjp(
        lambda raw_input: prepare(raw_input, q_gain, positions), query_f
    )
    key_full, key_back = jax.vjp(lambda raw_input: prepare(raw_input, k_gain, positions), key_f)
    query_prep = query_full.astype(jnp.bfloat16)
    key_flat = key_full.astype(jnp.bfloat16).reshape(tok_rows, kv_cols)
    pieces = [
        from_behind((key_flat, values), "seq", distance) for distance in range(halo_devices, 0, -1)
    ]
    key_ext = jnp.concatenate([piece[0] for piece in pieces] + [key_flat], axis=0)
    value_ext = jnp.concatenate([piece[1] for piece in pieces] + [values], axis=0)
    row_index = jnp.arange(tok_rows, dtype=jnp.int32)[:, None]
    col_index = jnp.arange(span_rows, dtype=jnp.int32)[None, :]
    gap = row_index - col_index + ext_rows
    key_pos = offset - ext_rows + col_index
    allowed = (key_pos >= 0) & (gap >= 0) & (gap < WINDOW)
    query_heads = query_prep.transpose(1, 0, 2)
    grad_heads = d_out.reshape(tok_rows, heads_q, head_dim).transpose(1, 0, 2)
    key_rep = jnp.repeat(
        key_ext.reshape(span_rows, heads_kv, head_dim).transpose(1, 0, 2), group_size, axis=0
    )
    value_rep = jnp.repeat(
        value_ext.reshape(span_rows, heads_kv, head_dim).transpose(1, 0, 2), group_size, axis=0
    )
    attn_heads, query_grads, key_grads, value_grads = lax.map(
        lambda items: head_core(items[0], items[1], items[2], items[3], allowed),
        (query_heads, key_rep, value_rep, grad_heads),
    )
    key_sum = (
        key_grads.reshape(heads_kv, group_size, span_rows, head_dim)
        .sum(axis=1)
        .transpose(1, 0, 2)
        .reshape(span_rows, kv_cols)
    )
    value_sum = (
        value_grads.reshape(heads_kv, group_size, span_rows, head_dim)
        .sum(axis=1)
        .transpose(1, 0, 2)
        .reshape(span_rows, kv_cols)
    )
    key_total = key_sum[ext_rows:]
    value_total = value_sum[ext_rows:]
    for distance in range(1, halo_devices + 1):
        block_start = (halo_devices - distance) * tok_rows
        back_key, back_value = from_behind(
            (
                key_sum[block_start : block_start + tok_rows],
                value_sum[block_start : block_start + tok_rows],
            ),
            "seq",
            -distance,
        )
        key_total = key_total + back_key
        value_total = value_total + back_value
    query_grad_prep = query_grads.transpose(1, 0, 2)
    query_grad = query_back(query_grad_prep)[0].reshape(tok_rows, q_cols).astype(jnp.bfloat16)
    key_grad = (
        key_back(key_total.reshape(tok_rows, heads_kv, head_dim))[0]
        .reshape(tok_rows, kv_cols)
        .astype(jnp.bfloat16)
    )
    value_grad = value_total.astype(jnp.bfloat16)
    attn_out = attn_heads.transpose(1, 0, 2).reshape(tok_rows, q_cols)
    grads_joined = jnp.concatenate([query_grad, key_grad, value_grad], axis=1)
    input_side = jnp.dot(x_sketch.T, grads_joined, preferred_element_type=jnp.float32)
    output_side = jnp.dot(dy_sketch.T, attn_out, preferred_element_type=jnp.float32)
    sketches = lax.psum_scatter(
        jnp.concatenate([input_side, output_side], axis=1), "seq", scatter_dimension=0, tiled=True
    )
    sketch_q = sketches[:, :q_cols]
    sketch_k = sketches[:, q_cols : q_cols + kv_cols]
    sketch_v = sketches[:, q_cols + kv_cols : q_cols + 2 * kv_cols]
    sketch_o = sketches[:, q_cols + 2 * kv_cols :]
    return (query_grad, key_grad, value_grad, sketch_q, sketch_k, sketch_v, sketch_o)


def solution(mesh):
    in_specs = (
        P("seq", "head"),
        P("head", None),
        P("seq", "head"),
        P("head", None),
        P("seq", "head"),
        P("seq", "head"),
        P("seq", "head"),
        P("seq", "head"),
        P(),
        P(),
    )
    out_specs = (
        P("seq", "head"),
        P("seq", "head"),
        P("seq", "head"),
        P("seq", "head"),
        P("seq", "head"),
        P("seq", "head"),
        P("seq", "head"),
    )
    return jax.shard_map(
        per_device, mesh=mesh, in_specs=in_specs, out_specs=out_specs, check_vma=False
    )
```

profile of v0, /device:TPU:0, one launch (start us, length us, event | category | flops | bytes accessed | tf_op | source)
XLA Modules:
  0.0 791.6 jit_solution(3361765780317403073)
XLA Ops:
  21.9 5.9 collective-permute-start
  27.8 4.4 collective-permute-start.1
  34.6 4.4 collective-permute-start.3
  39.0 3.9 copy.112
  45.0 3.9 copy.119
  56.3 5.3 all-reduce.6
  61.6 34.0 %collective-permute-done = bf16[512,1024]{1,0:T(8,128)(2,1)} collective-permute-done((bf16[512,1024]{1,0:T(8,128)(2,1)}, bf16[512,1024]{1,0:T(8,128)(2,1)}, u32[]{:S(2)}, u32[]{:S(2)}) %collective-permute-start) | collective-permute-done | bytes 1048608 | tf_op jit(solution)/shard_map/ppermute | solution.py:17
  98.7 15.7 %maximum_bitcast_fusion = bf16[8,1536,128]{2,0,1:T(8,128)(2,1)S(1)} fusion(bf16[512,8,128]{2,1,0:T(8,128)(2,1)S(1)} %copy-done.6, bf16[512,8,128]{2,1,0:T(8,128)(2,1)S(1)} %bitcast.158, bf16[512,8,128]{2,1,0:T(8,128)(2,1)S(1)} %bitcast.157), kind=kLoop, calls=%fused_computation.66 | loop fusion | flops 3145728 | bytes 6291456 | tf_op jit(solution)/shard_map/transpose | solution.py:99
  116.9 2.5 maximum_bitcast_fusion.1
  120.7 3.9 broadcast_in_dim.55
  124.6 3.9 broadcast_in_dim.56
  128.5 252.3 %while.17 = (s32[]{:T(128)}, bf16[16,512,128]{1,2,0:T(8,128)(2,1)}, f32[16,512,128]{1,2,0:T(8,128)}, f32[16,1536,128]{2,1,0:T(8,128)}, f32[16,1536,128]{2,1,0:T(...) while((s32[]{:T(128)}, bf16[16,512,128]{1,2,0:T(8,128)(2,1)}, ...), condition=%wide.region_5.6_spmd.clone, body=%wide.region_2.5_spmd.clone.sunk | while | flops 1224014848 | bytes 32396908 | solution.py:104
  135.4 2.6 fusion.101
  148.8 2.5 fusion.100
  151.3 2.5 fusion.101
  167.0 2.5 fusion.101
  182.8 2.5 fusion.101
  198.5 2.5 fusion.101
  214.2 2.5 fusion.101
  230.0 2.5 fusion.101
  245.8 2.5 fusion.101
  261.5 2.5 fusion.101
  277.3 2.5 fusion.101
  293.0 2.5 fusion.101
  308.8 2.5 fusion.101
  324.5 2.5 fusion.101
  340.3 2.5 fusion.101
  356.0 2.5 fusion.101
  371.7 2.6 fusion.101
  380.8 12.8 %bitcast_reduce_fusion = (f32[8,1536,128]{2,1,0:T(8,128)}, f32[8,1536,128]{2,1,0:T(8,128)S(1)}) fusion(f32[16,1536,128]{2,1,0:T(8,128)} %get-tuple-element.64, f32[16,1536,128]{2,1,0:T(8,128)} %get-tuple-element.63), kind=kLoop, calls=%fused_computation.48 | loop fusion | flops 3145728 | bytes 37748736 | tf_op jit(solution)/shard_map/reduce_sum | solution.py:116
  396.1 2.9 copy.124
  400.3 3.0 copy.125
  404.5 5.6 fusion.59
  410.1 2.9 copy.131
  414.4 3.0 copy.132
  418.7 3.0 multiply_add_fusion.3
  425.8 3.1 copy.130
  430.8 19.0 %collective-permute-done.4 = f32[512,1024]{0,1:T(8,128)} collective-permute-done((f32[512,1024]{0,1:T(8,128)}, f32[512,1024]{0,1:T(8,128)}, u32[]{:S(2)}, u32[]{:S(2)}) %collective-permute-start.4) | collective-permute-done | bytes 2097184 | tf_op jit(solution)/shard_map/ppermute | solution.py:17
  449.8 5.3 collective-permute-done.5
  455.1 3.6 fusion.51
  462.9 2.7 multiply_add_fusion.1
  466.9 3.6 multiply_reduce_fusion.1
  472.5 4.2 fusion.48
  480.2 12.4 %collective-permute-done.6 = f32[512,1024]{0,1:T(8,128)} collective-permute-done((f32[512,1024]{0,1:T(8,128)}, f32[512,1024]{0,1:T(8,128)}, u32[]{:S(2)}, u32[]{:S(2)}) %collective-permute-start.6) | collective-permute-done | bytes 2097184 | tf_op jit(solution)/shard_map/ppermute | solution.py:17
  492.6 5.6 collective-permute-done.7
  498.3 2.9 fusion.50
  504.6 4.1 copy.135
  511.0 270.4 %reduce-scatter.2.cloned.1.call-done = f32[8,6144]{1,0:T(8,128)} async-done(((f32[128,6144]{1,0:T(8,128)}), f32[8,6144]{1,0:T(8,128)}) %reduce-scatter.2.cloned.1.call-update) | async-done | bytes 196624 | tf_op jit(solution)/shard_map/reduce_scatter | solution.py:146
  (286 shorter events, 274.7 us)
Async XLA Ops:
  7.2 41.8 %copy-start = (bf16[512,2688]{1,0:T(8,128)(2,1)S(1)}, bf16[512,2688]{1,0:T(8,128)(2,1)}, u32[]{:S(2)}) copy-start(bf16[512,2688]{1,0:T(8,128)(2,1)} %param.12) | copy-start | bytes 8257540
  7.2 774.2 %reduce-scatter.2.cloned.1.call-start = ((), (), s32[]{:S(2)}) async-start(), calls=%async_computation.1 | async-start | bytes 3342336 | tf_op jit(solution)/shard_map/reduce_scatter | solution.py:146
  10.7 5.5 copy-start.31
  13.0 1.4 copy-start.27
  13.2 5.1 copy-start.11
  14.4 0.6 copy-start.16
  15.1 3.2 copy-start.13
  16.2 2.1 copy-start.15
  19.7 1.0 copy-start.5
  21.9 73.7 %collective-permute-start = (bf16[512,1024]{1,0:T(8,128)(2,1)}, bf16[512,1024]{1,0:T(8,128)(2,1)}, u32[]{:S(2)}, u32[]{:S(2)}) collective-permute-start(bf16[512,1024]{1,0:T(8,128)(2,1)} %bitcast.115), channel_id=1, source_target_pairs={{0,4},{2,6},{4,8},{6,10},{8,12},{10,14},{12,16},{14,18},{16,20},{1... | collective-permute-start | bytes 3145736 | tf_op jit(solution)/shard_map/ppermute | solution.py:17
  27.8 69.4 %collective-permute-start.1 = (bf16[512,1024]{1,0:T(8,128)(2,1)}, bf16[512,1024]{1,0:T(8,128)(2,1)}, u32[]{:S(2)}, u32[]{:S(2)}) collective-permute-start(bf16[512,1024]{1,0:T(8,128)(2,1)} %bitcast.115), channel_id=1, source_target_pairs={{0,2},{2,4},{4,6},{6,8},{8,10},{10,12},{12,14},{14,16},{16,18},{18... | collective-permute-start | bytes 3145736 | tf_op jit(solution)/shard_map/ppermute | solution.py:17
  32.2 84.7 %collective-permute-start.2 = (bf16[512,1024]{1,0:T(8,128)(2,1)}, bf16[512,1024]{1,0:T(8,128)(2,1)}, u32[]{:S(2)}, u32[]{:S(2)}) collective-permute-start(bf16[512,1024]{1,0:T(8,128)(2,1)} %param.18), channel_id=1, source_target_pairs={{0,4},{2,6},{4,8},{6,10},{8,12},{10,14},{12,16},{14,18},{16,20},{1... | collective-permute-start | bytes 3145736 | tf_op jit(solution)/shard_map/ppermute | solution.py:17
  34.6 82.3 %collective-permute-start.3 = (bf16[512,1024]{1,0:T(8,128)(2,1)}, bf16[512,1024]{1,0:T(8,128)(2,1)}, u32[]{:S(2)}, u32[]{:S(2)}) collective-permute-start(bf16[512,1024]{1,0:T(8,128)(2,1)} %param.18), channel_id=1, source_target_pairs={{0,2},{2,4},{4,6},{6,8},{8,10},{10,12},{12,14},{14,16},{16,18},{18... | collective-permute-start | bytes 3145736 | tf_op jit(solution)/shard_map/ppermute | solution.py:17
  45.0 4.0 copy-start.25
  45.0 6.1 copy-start.23
  49.0 2.2 copy-start.30
  49.0 2.2 copy-start.2
  51.2 1.8 copy-start.10
  51.2 1.9 copy-start.22
  53.1 0.9 copy-start.17
  53.1 1.0 copy-start.18
  95.6 3.1 copy-start.6
  399.0 50.8 %collective-permute-start.4 = (f32[512,1024]{0,1:T(8,128)}, f32[512,1024]{0,1:T(8,128)}, u32[]{:S(2)}, u32[]{:S(2)}) collective-permute-start(f32[512,1024]{0,1:T(8,128)} %bitcast.163), channel_id=1, source_target_pairs={{2,0},{4,2},{6,4},{8,6},{10,8},{12,10},{14,12},{16,14},{18,16},{20... | collective-permute-start | bytes 6291464 | tf_op jit(solution)/shard_map/ppermute | solution.py:17
  403.2 51.9 %collective-permute-start.5 = (f32[512,1024]{0,1:T(8,128)}, f32[512,1024]{0,1:T(8,128)}, u32[]{:S(2)}, u32[]{:S(2)}) collective-permute-start(f32[512,1024]{0,1:T(8,128)} %bitcast.164), channel_id=1, source_target_pairs={{4,0},{6,2},{8,4},{10,6},{12,8},{14,10},{16,12},{18,14},{20,16},{2... | collective-permute-start | bytes 6291464 | tf_op jit(solution)/shard_map/ppermute | solution.py:17
  413.1 79.6 %collective-permute-start.6 = (f32[512,1024]{0,1:T(8,128)}, f32[512,1024]{0,1:T(8,128)}, u32[]{:S(2)}, u32[]{:S(2)}) collective-permute-start(f32[512,1024]{0,1:T(8,128)} %bitcast.160), channel_id=1, source_target_pairs={{2,0},{4,2},{6,4},{8,6},{10,8},{12,10},{14,12},{16,14},{18,16},{20... | collective-permute-start | bytes 6291464 | tf_op jit(solution)/shard_map/ppermute | solution.py:17
  414.4 4.3 copy-start.19
  417.4 80.9 %collective-permute-start.7 = (f32[512,1024]{0,1:T(8,128)}, f32[512,1024]{0,1:T(8,128)}, u32[]{:S(2)}, u32[]{:S(2)}) collective-permute-start(f32[512,1024]{0,1:T(8,128)} %bitcast.161), channel_id=1, source_target_pairs={{4,0},{6,2},{8,4},{10,6},{12,8},{14,10},{16,12},{18,14},{20,16},{2... | collective-permute-start | bytes 6291464 | tf_op jit(solution)/shard_map/ppermute | solution.py:17
  418.7 3.0 copy-start.3
  421.7 0.8 copy-start.26
  421.7 0.8 copy-start.24
  422.6 2.4 copy-start.20
  422.6 2.4 copy-start.29
  461.0 2.0 copy-start.14
  465.6 1.3 copy-start.4
  466.9 4.7 copy-start.28
  466.9 5.5 copy-start.12
  476.7 21.6 %copy-start.7 = (f32[512,8,128]{0,2,1:T(8,128)S(1)}, f32[512,8,128]{0,2,1:T(8,128)}, u32[]{:S(2)}) copy-start(f32[512,8,128]{0,2,1:T(8,128)} %copy.130) | copy-start | bytes 6291460
  480.2 21.0 %copy-start.8 = (bf16[512,16,128]{0,2,1:T(8,128)(2,1)S(1)}, bf16[512,16,128]{0,2,1:T(8,128)(2,1)}, u32[]{:S(2)}) copy-start(bf16[512,16,128]{0,2,1:T(8,128)(2,1)} %fusion.38) | copy-start | bytes 6291460
  480.2 21.0 %copy-start.21 = (bf16[512,1024]{0,1:T(8,128)(2,1)S(1)}, bf16[512,1024]{0,1:T(8,128)(2,1)}, u32[]{:S(2)}) copy-start(bf16[512,1024]{0,1:T(8,128)(2,1)} %copy.133) | copy-start | bytes 3145732
  480.2 21.0 %copy-start.32 = (bf16[512,128]{1,0:T(8,128)(2,1)S(1)}, bf16[512,128]{1,0:T(8,128)(2,1)}, u32[]{:S(2)}) copy-start(bf16[512,128]{1,0:T(8,128)(2,1)} %get-tuple-element.212) | copy-start | bytes 393220
  501.2 1.5 copy-start.9
  504.6 279.7 %copy-start.1 = (bf16[512,2688]{1,0:T(8,128)(2,1)S(1)}, bf16[512,2688]{1,0:T(8,128)(2,1)}, u32[]{:S(2)}) copy-start(bf16[512,2688]{1,0:T(8,128)(2,1)} %param.12) | copy-start | bytes 8257540
Sparse Core Ops, SparseCore 0:
  504.7 276.5 reduce-scatter.1
where the time goes:
time: 802 us; the launch traced here: 792 us
  waiting for transfers between devices  349 us (44%)
  matrix products  196 us (24%)
  local copies, waits for them, and re-layouts  125 us (16%)
  other arithmetic  77.9 us (10%)
  starting transfers between devices  22.2 us (3%)
  between operations  15.1 us (2%)
    reduce_scatter x1, waiting for transfers between devices, per_device(): lax.psum_scatter(jnp.concatenate([input_side, output_side], axis=1), 'seq...  270 us
    ppermute x8, waiting for transfers between devices, from_behind(): return lax.ppermute(shard, axis, pairs)  78.4 us
    dynamic_update_slice x64, local copies, waits for them, and re-layouts, per_device(): lax.map(lambda items: head_core(items[0], items[1], items[2], items[3], a...  52.7 us
    dot_general x16, matrix products, head_core(): jnp.dot(probs_low.T, grad_rows, preferred_element_type=jnp.float32)  40.4 us
    dot_general x16, matrix products, head_core(): jnp.dot(grad_low.T, query_rows, preferred_element_type=jnp.float32)  38.9 us
    dot_general x16, matrix products, head_core(): jnp.dot(query_rows, key_rows.T, preferred_element_type=jnp.float32)  30.8 us
    unnamed x78, local copies, waits for them, and re-layouts  30.6 us
    dot_general x16, matrix products, head_core(): jnp.dot(grad_rows, value_rows.T, preferred_element_type=jnp.float32)  29.7 us
  transfers between devices with their start and end apart: 9, of which 7 were waited for; matrix products, arithmetic and copies ran while one was open for 12% of the time, Pallas kernels for 0%

commit v1 on v0

v1 whole, which is shorter than its diff:
```python
import functools
import math

import jax
import jax.numpy as jnp
from jax import lax
from jax.experimental import pallas as pl
from jax.experimental.pallas import tpu as pltpu
from jax.sharding import PartitionSpec as P

WINDOW = 1024
SCALE = 168.0 ** (-0.5)
EPSILON = 1e-06
ROPE_BASE = 10000.0
NT = (((1,), (1,)), ((), ()))
CHUNKS = 2


def from_behind(shard, axis, by):
    count = lax.axis_size(axis)
    pairs = [(i, i + by) for i in range(count) if 0 <= i + by < count]
    return lax.ppermute(shard, axis, pairs)


def dot(a, b):
    return jnp.dot(a, b, preferred_element_type=jnp.float32)


def dot_nt(a, b):
    return lax.dot_general(a, b, NT, preferred_element_type=jnp.float32)


def swap_halves(x):
    return pltpu.roll(x, x.shape[-1] // 2, 1)


def norm_parts(raw):
    rstd = lax.rsqrt(jnp.mean(raw * raw, axis=-1, keepdims=True) + EPSILON)
    return raw * rstd, rstd


def rotate(normed, cos, sin):
    return normed * cos + swap_halves(normed) * sin


def prepare_back(grad, unit, rstd, gain, cos, sin):
    inner = (grad * cos + swap_halves(grad * sin)) * gain
    return rstd * (inner - unit * jnp.mean(inner * unit, axis=-1, keepdims=True))


def attention_kernel(
    valid, cos, sin, q_gain, k_gain, x_t, dy_t, q, d_out, near, far, k_own, v_own, *rest
):
    (query_out, own_out, near_out, far_out, sketch_out, k_s, v_s, kt_s, vt_s, dk_s, dv_s,
     e_s, dp_s, p_s, ds_s) = rest[-15:]
    tok = q.shape[0]
    hd = q_gain.shape[1]
    group = q.shape[1] // hd
    sub = tok // 2
    span = 3 * tok
    band = 5 * sub
    cols = group * sub
    exponent = SCALE * math.log2(math.e)

    for part, raw, val in ((0, far[0], far[1]), (1, near[0], near[1]), (2, k_own[...], v_own[...])):
        rows = pl.ds(part * tok, tok)
        unit, _ = norm_parts(raw.astype(jnp.float32))
        prep = rotate(unit * k_gain[...], cos[rows, :], sin[rows, :])
        k_s[rows, :] = prep.astype(jnp.bfloat16)
        kt_s[:, part * tok : (part + 1) * tok] = prep.T.astype(jnp.bfloat16)
        v_s[rows, :] = val
        vt_s[:, part * tok : (part + 1) * tok] = val.astype(jnp.float32).T.astype(jnp.bfloat16)

    key_at = lax.broadcasted_iota(jnp.int32, (sub, cols), 0)
    query_at = lax.broadcasted_iota(jnp.int32, (sub, cols), 1) % sub
    older = key_at > query_at
    weight = jnp.where(older, valid[1], 1.0)

    for i in range(2):
        rows = slice(i * sub, (i + 1) * sub)
        own_rows = pl.ds(2 * tok + i * sub, sub)
        q_cos, q_sin = cos[own_rows, :], sin[own_rows, :]
        units = []
        preps = []
        for h in range(group):
            unit, rstd = norm_parts(q[rows, h * hd : (h + 1) * hd].astype(jnp.float32))
            units.append((unit, rstd))
            preps.append(rotate(unit * q_gain[...], q_cos, q_sin).astype(jnp.bfloat16))
        query = jnp.concatenate(preps, axis=0)
        grad = jnp.concatenate([d_out[rows, h * hd : (h + 1) * hd] for h in range(group)], axis=0)

        total = jnp.zeros((1, cols), jnp.float32)
        mixed = jnp.zeros((1, cols), jnp.float32)
        for t in range(4):
            at = slice((i + t) * sub, (i + t + 1) * sub)
            score = dot_nt(k_s[at, :], query)
            grad_p = dot_nt(v_s[at, :], grad)
            if t == 0:
                last = slice((i + 4) * sub, (i + 5) * sub)
                score = jnp.where(older, score, dot_nt(k_s[last, :], query))
                grad_p = jnp.where(older, grad_p, dot_nt(v_s[last, :], grad))
            e = jnp.exp2(score * exponent)
            here = slice(t * sub, (t + 1) * sub)
            e_s[i, here, :] = e
            dp_s[i, here, :] = grad_p
            mixed = mixed + jnp.sum(e * grad_p, axis=0, keepdims=True)
            if t == 0:
                total = total + jnp.sum(e * weight, axis=0, keepdims=True)
            else:
                part = jnp.sum(e, axis=0, keepdims=True)
                shard = (i + t) // 2
                total = total + (part if shard == 2 else part * valid[1 - shard])
        inverse = 1.0 / total
        delta = mixed * inverse
        for t in range(4):
            here = slice(t * sub, (t + 1) * sub)
            prob = e_s[i, here, :] * inverse
            ds = prob * (dp_s[i, here, :] - delta)
            if t == 0:
                last = slice(4 * sub, 5 * sub)
                p_s[i, here, :] = jnp.where(older, prob, 0.0).astype(jnp.bfloat16)
                p_s[i, last, :] = jnp.where(older, 0.0, prob).astype(jnp.bfloat16)
                ds_s[i, here, :] = jnp.where(older, ds, 0.0).astype(jnp.bfloat16)
                ds_s[i, last, :] = jnp.where(older, 0.0, ds).astype(jnp.bfloat16)
            else:
                p_s[i, here, :] = prob.astype(jnp.bfloat16)
                ds_s[i, here, :] = ds.astype(jnp.bfloat16)

        keys = slice(i * sub, i * sub + band)
        dv = dot(p_s[i], grad)
        dk = dot(ds_s[i], query)
        if i == 0:
            dv_s[:band, :] = dv
            dk_s[:band, :] = dk
            dv_s[band:, :] = jnp.zeros((span - band, hd), jnp.float32)
            dk_s[band:, :] = jnp.zeros((span - band, hd), jnp.float32)
        else:
            dv_s[keys, :] += dv
            dk_s[keys, :] += dk
        attn_t = dot(vt_s[:, keys], p_s[i]).astype(jnp.bfloat16)
        dq = dot(kt_s[:, keys], ds_s[i]).T * SCALE
        for h in range(group):
            unit, rstd = units[h]
            part = prepare_back(
                dq[h * sub : (h + 1) * sub, :], unit, rstd, q_gain[...], q_cos, q_sin
            ).astype(jnp.bfloat16)
            query_out[rows, h * hd : (h + 1) * hd] = part
            sk_q = dot(x_t[:, 2 * tok + i * sub : 2 * tok + (i + 1) * sub], part)
            sk_o = dot_nt(dy_t[:, rows], attn_t[:, h * sub : (h + 1) * sub])
            to_q = slice(h * hd, (h + 1) * hd)
            to_o = slice((group + 2 + h) * hd, (group + 3 + h) * hd)
            if i == 0:
                sketch_out[0, :, to_q] = sk_q
                sketch_out[0, :, to_o] = sk_o
            else:
                sketch_out[0, :, to_q] += sk_q
                sketch_out[0, :, to_o] += sk_o

    sk_k = jnp.zeros((x_t.shape[0], hd), jnp.float32)
    sk_v = jnp.zeros((x_t.shape[0], hd), jnp.float32)
    for part, raw, out in ((0, far[0], far_out), (1, near[0], near_out), (2, k_own[...], own_out)):
        rows = pl.ds(part * tok, tok)
        unit, rstd = norm_parts(raw.astype(jnp.float32))
        dk = prepare_back(
            dk_s[rows, :] * SCALE, unit, rstd, k_gain[...], cos[rows, :], sin[rows, :]
        )
        dv = dv_s[rows, :]
        out[0] = dk.astype(out.dtype)
        out[1] = dv.astype(out.dtype)
        xs = x_t[:, part * tok : (part + 1) * tok]
        sk_k = sk_k + dot(xs, dk.astype(jnp.bfloat16))
        sk_v = sk_v + dot(xs, dv.astype(jnp.bfloat16))
    sketch_out[0, :, group * hd : (group + 1) * hd] = sk_k
    sketch_out[0, :, (group + 1) * hd : (group + 2) * hd] = sk_v


def attention(chunk, heads, valid, cos, sin, q_gain, k_gain, x_t, dy_t, q_raw, d_out, near, far,
              k_raw, values, earlier):
    tok, q_cols = q_raw.shape
    hd = q_gain.shape[1]
    group = q_cols // k_raw.shape[1]
    rank = x_t.shape[0]
    wide = group * hd
    first = chunk * heads
    span, sub = 3 * tok, tok // 2
    whole = lambda *shape: pl.BlockSpec(shape, lambda g: (0,) * len(shape))
    q_spec = pl.BlockSpec((tok, wide), lambda g: (0, first + g))
    k_spec = pl.BlockSpec((tok, hd), lambda g: (0, first + g))
    halo = pl.BlockSpec((2, tok, hd), lambda g: (0, 0, g))
    in_specs = [
        pl.BlockSpec(memory_space=pltpu.SMEM),
        whole(span, hd), whole(span, hd), whole(1, hd), whole(1, hd),
        whole(rank, span), whole(rank, tok),
        q_spec, q_spec, halo, halo, k_spec, k_spec,
    ]
    args = [valid, cos, sin, q_gain, k_gain, x_t, dy_t, q_raw, d_out, near, far, k_raw, values]
    aliases = {}
    if earlier is not None:
        in_specs.append(pl.BlockSpec(memory_space=pl.ANY))
        aliases = {len(args): 0}
        args.append(earlier)
    cols = group * sub
    return pl.pallas_call(
        attention_kernel,
        grid=(heads,),
        in_specs=in_specs,
        out_specs=[q_spec, halo, halo, halo,
                   pl.BlockSpec((1, rank, 2 * wide + 2 * hd), lambda g: (g, 0, 0))],
        out_shape=[
            jax.ShapeDtypeStruct(q_raw.shape, jnp.bfloat16),
            jax.ShapeDtypeStruct((2, tok, heads * hd), jnp.float32),
            jax.ShapeDtypeStruct((2, tok, heads * hd), jnp.bfloat16),
            jax.ShapeDtypeStruct((2, tok, heads * hd), jnp.bfloat16),
            jax.ShapeDtypeStruct((heads, rank, 2 * wide + 2 * hd), jnp.float32),
        ],
        scratch_shapes=[
            pltpu.VMEM((span, hd), jnp.bfloat16),
            pltpu.VMEM((span, hd), jnp.bfloat16),
            pltpu.VMEM((hd, span), jnp.bfloat16),
            pltpu.VMEM((hd, span), jnp.bfloat16),
            pltpu.VMEM((span, hd), jnp.float32),
            pltpu.VMEM((span, hd), jnp.float32),
            pltpu.VMEM((2, 4 * sub, cols), jnp.float32),
            pltpu.VMEM((2, 4 * sub, cols), jnp.float32),
            pltpu.VMEM((2, 5 * sub, cols), jnp.bfloat16),
            pltpu.VMEM((2, 5 * sub, cols), jnp.bfloat16),
        ],
        input_output_aliases=aliases,
        compiler_params=pltpu.CompilerParams(
            dimension_semantics=("arbitrary",), vmem_limit_bytes=48 * 1024 * 1024
        ),
        cost_estimate=pl.CostEstimate(
            flops=heads * 20 * 5 * sub * tok * group * hd,
            bytes_accessed=heads * 4 * tok * hd * 20,
            transcendentals=heads * 4 * sub * tok * group,
        ),
    )(*args)


def scatter_sum(part, order):
    count = lax.axis_size("seq")
    bits = len(order)
    heads, rank, cols = part.shape
    me = lax.axis_index("seq")
    cur = part.reshape((heads,) + (2,) * bits + (rank // count, cols))
    axes = list(range(bits - 1, -1, -1))
    for bit in order:
        axis = 1 + axes.index(bit)
        axes.remove(bit)
        mine = (me >> bit) & 1
        keep = lax.dynamic_index_in_dim(cur, mine, axis, keepdims=False)
        away = lax.dynamic_index_in_dim(cur, 1 - mine, axis, keepdims=False)
        pairs = [(i, i ^ (1 << bit)) for i in range(count)]
        cur = keep + lax.ppermute(away.astype(jnp.bfloat16), "seq", pairs).astype(jnp.float32)
    return cur


def per_device(
    layer_input, omega_in, upstream, omega_out, q_raw, k_raw, values, d_out, q_gain, k_gain
):
    tok = q_raw.shape[0]
    hd = q_gain.shape[0]
    kv_cols = k_raw.shape[1]
    heads_kv = kv_cols // hd
    group = q_raw.shape[1] // kv_cols
    per_chunk = heads_kv // CHUNKS
    c_cols = per_chunk * hd
    me = lax.axis_index("seq")
    count = lax.axis_size("seq")

    halos = []
    for c in range(CHUNKS):
        pair = jnp.stack([k_raw[:, c * c_cols : (c + 1) * c_cols],
                          values[:, c * c_cols : (c + 1) * c_cols]])
        halos.append((from_behind(pair, "seq", 1), from_behind(pair, "seq", 2)))

    partial_x = dot(layer_input, omega_in)
    partial_y = dot(upstream, omega_out)
    summed_x, summed_y = lax.psum((partial_x, partial_y), "head")
    x_sketch = summed_x.astype(jnp.bfloat16)
    dy_t = summed_y.astype(jnp.bfloat16).T
    x_t = x_sketch.T
    x_t = jnp.concatenate([from_behind(x_t, "seq", 2), from_behind(x_t, "seq", 1), x_t], axis=1)

    half = hd // 2
    inverse_freq = ROPE_BASE ** (-(jnp.arange(half, dtype=jnp.float32) * 2.0 / hd))
    positions = (me - 2) * tok + jnp.arange(3 * tok, dtype=jnp.int32)
    angles = positions.astype(jnp.float32)[:, None] * inverse_freq[None, :]
    cos, sin = jnp.cos(angles), jnp.sin(angles)
    cos = jnp.concatenate([cos, cos], axis=1)
    sin = jnp.concatenate([-sin, sin], axis=1)
    valid = jnp.stack([me >= 1, me >= 2]).astype(jnp.float32)

    query_grad = None
    returned = []
    sketches = []
    bits = count.bit_length() - 1
    for c in range(CHUNKS):
        query_grad, own, near, far, sketch = attention(
            c, per_chunk, valid, cos, sin, q_gain[None, :], k_gain[None, :], x_t, dy_t,
            q_raw, d_out, halos[c][0], halos[c][1], k_raw, values, query_grad,
        )
        back = (own, from_behind(near, "seq", -1), from_behind(far, "seq", -2))
        returned.append(back)
        order = list(range(bits))
        if c % 2 == 1 and bits > 1:
            order[0], order[1] = order[1], order[0]
        sketches.append(scatter_sum(sketch, order))

    sums = [(o + n.astype(jnp.float32) + f.astype(jnp.float32)).astype(jnp.bfloat16)
            for o, n, f in returned]
    key_grad = jnp.concatenate([s[0] for s in sums], axis=1)
    value_grad = jnp.concatenate([s[1] for s in sums], axis=1)
    all_sketch = jnp.concatenate(sketches, axis=0)

    def columns(first, width):
        piece = all_sketch[:, :, first : first + width]
        return piece.transpose(1, 0, 2).reshape(piece.shape[1], heads_kv * width)

    wide = group * hd
    return (
        query_grad, key_grad, value_grad,
        columns(0, wide), columns(wide, hd), columns(wide + hd, hd), columns(wide + 2 * hd, wide),
    )


def solution(mesh):
    split = P("seq", "head")
    by_head = P("head", None)
    in_specs = (split, by_head, split, by_head, split, split, split, split, P(), P())
    return jax.shard_map(
        per_device, mesh=mesh, in_specs=in_specs, out_specs=(split,) * 7, check_vma=False
    )
```

time: 802 us -> 318 us (0.40); the launches traced: 792 us -> 317 us
  waiting for transfers between devices: 349 us -> 118 us
  matrix products: 196 us -> 3.22 us
  local copies, waits for them, and re-layouts: 125 us -> 14.3 us
  Pallas kernels: 0 us -> 71.2 us
  starting transfers between devices: 22.2 us -> 90.6 us
  other arithmetic: 77.9 us -> 13.4 us
  between operations: 15.1 us -> 0.96 us
    reduce_scatter x1 -> x0, waiting for transfers between devices: 270 us -> none  [per_device(): lax.psum_scatter(jnp.concatenate([input_side, output_side], axis=1), 'seq...]
    dot_general x100 -> x2, matrix products: 196 us -> 3.22 us  [dot(): return jnp.dot(a, b, preferred_element_type=jnp.float32)]
    pallas_call x0 -> x2, Pallas kernels: none -> 71.2 us  [attention(): pl.pallas_call(attention_kernel, grid=(heads,), in_specs=in_specs, out_sp...]
    ppermute x0 -> x8, waiting for transfers between devices: none -> 66.7 us  [scatter_sum(): lax.ppermute(away.astype(jnp.bfloat16), 'seq', pairs).astype(jnp.float32)]
    ppermute x0 -> x8, starting transfers between devices: none -> 62.3 us  [scatter_sum(): lax.ppermute(away.astype(jnp.bfloat16), 'seq', pairs).astype(jnp.float32)]
    dynamic_update_slice x64 -> x0, local copies, waits for them, and re-layouts: 52.7 us -> none  [per_device(): lax.map(lambda items: head_core(items[0], items[1], items[2], items[3], a...]
    slice x10 -> x0, local copies, waits for them, and re-layouts: 27.7 us -> none  [the longest x2 8.75 us: per_device(): value_total = value_sum[ext_rows:]]
    ppermute x8 -> x10, waiting for transfers between devices: 78.4 us -> 50.9 us  [from_behind(): return lax.ppermute(shard, axis, pairs)]
  transfers between devices with their start and end apart: 9 -> 18, of which waited for: 7 -> 8; matrix products, arithmetic and copies ran while one was open for 12% -> 5% of each run, Pallas kernels for 0% -> 22%
where the time goes in v1:
time: 318 us; the launch traced here: 317 us
  waiting for transfers between devices  118 us (37%)
  starting transfers between devices  90.6 us (28%)
  Pallas kernels  71.2 us (22%)
  local copies, waits for them, and re-layouts  14.3 us (4%)
  other arithmetic  13.4 us (4%)
  blocking collectives  5.64 us (2%)
  matrix products  3.22 us (1%)
    pallas_call x2, Pallas kernels, attention(): pl.pallas_call(attention_kernel, grid=(heads,), in_specs=in_specs, out_sp...  71.2 us
    ppermute x8, waiting for transfers between devices, scatter_sum(): lax.ppermute(away.astype(jnp.bfloat16), 'seq', pairs).astype(jnp.float32)  66.7 us
    ppermute x8, starting transfers between devices, scatter_sum(): lax.ppermute(away.astype(jnp.bfloat16), 'seq', pairs).astype(jnp.float32)  62.3 us
    ppermute x10, waiting for transfers between devices, from_behind(): return lax.ppermute(shard, axis, pairs)  50.9 us
    ppermute x10, starting transfers between devices, from_behind(): return lax.ppermute(shard, axis, pairs)  28.2 us
    unnamed x28, local copies, waits for them, and re-layouts  9.23 us
  transfers between devices with their start and end apart: 18, of which 8 were waited for; matrix products, arithmetic and copies ran while one was open for 5% of the time, Pallas kernels for 22%

profile of v1, /device:TPU:0, one launch (start us, length us, event | category | flops | bytes accessed | tf_op | source)
XLA Modules:
  0.0 316.9 jit_solution(12303769838311938175)
XLA Ops:
  0.7 1.7 copy-done
  2.4 2.2 fusion.14
  4.6 1.0 fusion.15
  5.7 5.6 %all-reduce.2 = (bf16[512,128]{0,1:T(8,128)(2,1)}, bf16[512,128]{0,1:T(8,128)(2,1)}) all-reduce(f32[512,128]{0,1:T(8,128)S(1)} %fusion.14, f32[512,128]{0,1:T(8,128)S(1)} %fusion.15), channel_id=1, replica_groups=mesh['seq'=16,'head'=2] {'head'}, use_global_device_ids=true, to_apply=%region_0.0 | all-reduce | flops 131072 | bytes 786432 | tf_op jit(solution)/shard_map/psum | solution.py:279
  11.3 5.2 %collective-permute-start.1 = (bf16[128,512]{1,0:T(8,128)(2,1)}, bf16[128,512]{1,0:T(8,128)(2,1)}, u32[]{:S(2)}, u32[]{:S(2)}) collective-permute-start(bf16[128,512]{1,0:T(8,128)(2,1)} %bitcast.73), channel_id=1, source_target_pairs={{0,2},{2,4},{4,6},{6,8},{8,10},{10,12},{12,14},{14,16},{16,18},{18... | collective-permute-start | bytes 393224 | tf_op jit(solution)/shard_map/ppermute | solution.py:22
  16.5 3.4 %collective-permute-start = (bf16[128,512]{1,0:T(8,128)(2,1)}, bf16[128,512]{1,0:T(8,128)(2,1)}, u32[]{:S(2)}, u32[]{:S(2)}) collective-permute-start(bf16[128,512]{1,0:T(8,128)(2,1)} %bitcast.73), channel_id=1, source_target_pairs={{0,4},{2,6},{4,8},{6,10},{8,12},{10,14},{12,16},{14,18},{16,20},{1... | collective-permute-start | bytes 393224 | tf_op jit(solution)/shard_map/ppermute | solution.py:22
  19.9 1.7 slice_bitcast_fusion.4
  21.6 1.1 pad_maximum_fusion.1
  22.6 3.8 %collective-permute-start.5 = (bf16[2,512,512]{2,1,0:T(8,128)(2,1)}, bf16[2,512,512]{2,1,0:T(8,128)(2,1)}, u32[]{:S(2)}, u32[]{:S(2)}) collective-permute-start(bf16[2,512,512]{2,1,0:T(8,128)(2,1)} %pad_maximum_fusion.1), channel_id=1, source_target_pairs={{0,4},{2,6},{4,8},{6,10},{8,12},{10,14},{12,16},{14,18},{16,20},{1... | collective-permute-start | bytes 3145736 | tf_op jit(solution)/shard_map/ppermute | solution.py:22
  26.4 4.4 %collective-permute-start.4 = (bf16[2,512,512]{2,1,0:T(8,128)(2,1)}, bf16[2,512,512]{2,1,0:T(8,128)(2,1)}, u32[]{:S(2)}, u32[]{:S(2)}) collective-permute-start(bf16[2,512,512]{2,1,0:T(8,128)(2,1)} %pad_maximum_fusion.1), channel_id=1, source_target_pairs={{0,2},{2,4},{4,6},{6,8},{8,10},{10,12},{12,14},{14,16},{16,18},{18... | collective-permute-start | bytes 3145736 | tf_op jit(solution)/shard_map/ppermute | solution.py:22
  30.8 1.1 pad_maximum_fusion
  31.9 2.5 collective-permute-start.3
  34.4 2.8 fusion.2
  37.3 1.3 pad_maximum_fusion.4
  38.7 3.6 %collective-permute-start.2 = (bf16[2,512,512]{2,1,0:T(8,128)(2,1)}, bf16[2,512,512]{2,1,0:T(8,128)(2,1)S(1)}, u32[]{:S(2)}, u32[]{:S(2)}) collective-permute-start(bf16[2,512,512]{2,1,0:T(8,128)(2,1)} %pad_maximum_fusion), channel_id=1, source_target_pairs={{0,2},{2,4},{4,6},{6,8},{8,10},{10,12},{12,14},{14,16},{16,18},{18... | collective-permute-start | bytes 3145736 | tf_op jit(solution)/shard_map/ppermute | solution.py:22
  42.4 1.1 pad_maximum_fusion.6.x_t
  43.4 50.8 %collective-permute-done.5.far = bf16[2,512,512]{2,1,0:T(8,128)(2,1)} collective-permute-done((bf16[2,512,512]{2,1,0:T(8,128)(2,1)}, bf16[2,512,512]{2,1,0:T(8,128)(2,1)}, u32[]{:S(2)}, u32[]{:S(2)}) %collective-permute-start.5) | collective-permute-done | bytes 1048608 | tf_op jit(solution)/shard_map/ppermute | solution.py:22
  94.3 1.1 copy-done.1
  95.4 0.9 copy-done.6
  96.3 35.4 %shard_map.153 = (bf16[512,2048]{1,0:T(8,128)(2,1)}, f32[2,512,512]{2,1,0:T(8,128)}, bf16[2,512,512]{2,1,0:T(8,128)(2,1)S(1)}, bf16[2,512,512]{2,1,0:T(8,128)(2,1)S(1)}, f32[4,128,768]{2,1,0:T(8,128)}) custom-call(f32[2]{0:T(128)S(1)} %add_convert_fusion.3.valid, f32[1536,128]{1,0:T(8,128)S(1)} %get-tuple-element.44.cos, f32[1536,128]{1,0:T(8,128)S(1)} %copy-done.1, ...), custom_call_target="tpu_custom_call" | custom-call | flops 13421772800 | bytes 20971520 | tf_op jit(solution)/shard_map/pallas_call | solution.py:203
  131.8 1.0 copy-done.2
  132.7 1.0 copy-done.4
  133.7 1.9 fusion.1
  135.7 35.8 %shard_map.154 = (bf16[512,2048]{1,0:T(8,128)(2,1)}, f32[2,512,512]{2,1,0:T(8,128)}, bf16[2,512,512]{2,1,0:T(8,128)(2,1)S(1)}, bf16[2,512,512]{2,1,0:T(8,128)(2,1)S(1)}, f32[4,128,768]{2,1,0:T(8,128)}) custom-call(f32[2]{0:T(128)S(1)} %add_convert_fusion.3.valid, f32[1536,128]{1,0:T(8,128)S(1)} %get-tuple-element.44.cos, ...), custom_call_target="tpu_custom_call", output_to_operand_aliasing={{0}: (13, {})} | custom-call | flops 13421772800 | bytes 20971520 | tf_op jit(solution)/shard_map/pallas_call | solution.py:203
  171.4 1.0 copy-done.3
  172.4 1.0 copy-done.5
  173.4 1.2 fusion
  174.6 2.6 collective-permute-start.14
  177.1 1.4 collective-permute-start.6
  178.5 1.3 collective-permute-start.7
  179.8 1.3 collective-permute-start.8
  181.1 1.3 collective-permute-start.9
  182.4 1.3 bitcast_add_fusion.1
  183.8 1.9 collective-permute-done.14
  185.7 4.2 %collective-permute-start.11 = (bf16[4,2,2,8,768]{4,3,0,1,2:T(8,128)(2,1)S(1)}, bf16[4,2,2,8,768]{4,3,0,1,2:T(8,128)(2,1)S(1)}, u32[]{:S(2)}, u32[]{:S(2)}) collective-permute-start(bf16[4,2,2,8,768]{4,3,0,1,2:T(8,128)(2,1)S(1)} %fusion.3), channel_id=1, source_target_pairs={{0,4},{2,6},{4,0},{6,2},{8,12},{10,14},{12,8},{14,10},{16,20},{18,... | collective-permute-start | bytes 589832 | tf_op jit(solution)/shard_map/ppermute | solution.py:254
  190.0 43.2 %collective-permute-done.11 = bf16[4,2,2,8,768]{4,3,0,1,2:T(8,128)(2,1)S(1)} collective-permute-done((bf16[4,2,2,8,768]{4,3,0,1,2:T(8,128)(2,1)S(1)}, bf16[4,2,2,8,768]{4,3,0,1,2:T(8,128)(2,1)S(1)}, u32[]{:S(2)}, u32[]{:S(2)}) %collective-permute-start.11) | collective-permute-done | bytes 196640 | tf_op jit(solution)/shard_map/ppermute | solution.py:254
  233.2 49.9 %collective-permute-start.15 = (bf16[4,2,2,8,768]{4,3,2,1,0:T(8,128)(2,1)S(1)}, bf16[4,2,2,8,768]{4,3,2,1,0:T(8,128)(2,1)S(1)}, u32[]{:S(2)}, u32[]{:S(2)}) collective-permute-start(bf16[4,2,2,8,768]{4,3,2,1,0:T(8,128)(2,1)S(1)} %fusion.4), channel_id=1, source_target_pairs={{0,2},{2,0},{4,6},{6,4},{8,10},{10,8},{12,14},{14,12},{16,18},{18,... | collective-permute-start | bytes 589832 | tf_op jit(solution)/shard_map/ppermute | solution.py:254
  283.3 3.6 %collective-permute-done.15 = bf16[4,2,2,8,768]{4,3,2,1,0:T(8,128)(2,1)S(1)} collective-permute-done((bf16[4,2,2,8,768]{4,3,2,1,0:T(8,128)(2,1)S(1)}, bf16[4,2,2,8,768]{4,3,2,1,0:T(8,128)(2,1)S(1)}, u32[]{:S(2)}, u32[]{:S(2)}) %collective-permute-start.15) | collective-permute-done | bytes 196640 | tf_op jit(solution)/shard_map/ppermute | solution.py:254
  286.8 1.6 collective-permute-start.12
  288.5 7.1 %collective-permute-done.12 = bf16[4,2,8,768]{3,2,0,1:T(8,128)(2,1)S(1)} collective-permute-done((bf16[4,2,8,768]{3,2,0,1:T(8,128)(2,1)S(1)}, bf16[4,2,8,768]{3,2,0,1:T(8,128)(2,1)S(1)}, u32[]{:S(2)}, u32[]{:S(2)}) %collective-permute-start.12) | collective-permute-done | bytes 98336 | tf_op jit(solution)/shard_map/ppermute | solution.py:254
  295.6 5.1 %collective-permute-done.16 = bf16[4,2,8,768]{3,2,1,0:T(8,128)(2,1)S(1)} collective-permute-done((bf16[4,2,8,768]{3,2,1,0:T(8,128)(2,1)S(1)}, bf16[4,2,8,768]{3,2,1,0:T(8,128)(2,1)S(1)}, u32[]{:S(2)}, u32[]{:S(2)}) %collective-permute-start.16) | collective-permute-done | bytes 98336 | tf_op jit(solution)/shard_map/ppermute | solution.py:254
  300.7 2.0 collective-permute-start.13
  302.8 2.9 collective-permute-done.13
  305.7 2.0 collective-permute-start.17
  307.8 2.9 collective-permute-done.17
  312.6 1.5 copy-done.11
  314.6 1.1 pad_maximum_fusion.3
  315.7 1.1 pad_maximum_fusion.2
  (54 shorter events, 2.9 us)
Async XLA Ops:
  0.6 1.8 copy-start
  0.6 4.0 %copy-start.13 = (bf16[2688,128]{1,0:T(8,128)(2,1)S(1)}, bf16[2688,128]{1,0:T(8,128)(2,1)}, u32[]{:S(2)}) copy-start(bf16[2688,128]{1,0:T(8,128)(2,1)} %param.13) | copy-start | bytes 2064388
  0.7 4.0 %copy-start.9 = (bf16[512,2688]{1,0:T(8,128)(2,1)S(1)}, bf16[512,2688]{1,0:T(8,128)(2,1)}, u32[]{:S(2)}) copy-start(bf16[512,2688]{1,0:T(8,128)(2,1)} %param.12) | copy-start | bytes 8257540
  11.3 27.4 %collective-permute-start.1 = (bf16[128,512]{1,0:T(8,128)(2,1)}, bf16[128,512]{1,0:T(8,128)(2,1)}, u32[]{:S(2)}, u32[]{:S(2)}) collective-permute-start(bf16[128,512]{1,0:T(8,128)(2,1)} %bitcast.73), channel_id=1, source_target_pairs={{0,2},{2,4},{4,6},{6,8},{8,10},{10,12},{12,14},{14,16},{16,18},{18... | collective-permute-start | bytes 393224 | tf_op jit(solution)/shard_map/ppermute | solution.py:22
  16.5 25.8 %collective-permute-start = (bf16[128,512]{1,0:T(8,128)(2,1)}, bf16[128,512]{1,0:T(8,128)(2,1)}, u32[]{:S(2)}, u32[]{:S(2)}) collective-permute-start(bf16[128,512]{1,0:T(8,128)(2,1)} %bitcast.73), channel_id=1, source_target_pairs={{0,4},{2,6},{4,8},{6,10},{8,12},{10,14},{12,16},{14,18},{16,20},{1... | collective-permute-start | bytes 393224 | tf_op jit(solution)/shard_map/ppermute | solution.py:22
  22.6 71.6 %collective-permute-start.5 = (bf16[2,512,512]{2,1,0:T(8,128)(2,1)}, bf16[2,512,512]{2,1,0:T(8,128)(2,1)}, u32[]{:S(2)}, u32[]{:S(2)}) collective-permute-start(bf16[2,512,512]{2,1,0:T(8,128)(2,1)} %pad_maximum_fusion.1), channel_id=1, source_target_pairs={{0,4},{2,6},{4,8},{6,10},{8,12},{10,14},{12,16},{14,18},{16,20},{1... | collective-permute-start | bytes 3145736 | tf_op jit(solution)/shard_map/ppermute | solution.py:22
  26.4 67.8 %collective-permute-start.4 = (bf16[2,512,512]{2,1,0:T(8,128)(2,1)}, bf16[2,512,512]{2,1,0:T(8,128)(2,1)}, u32[]{:S(2)}, u32[]{:S(2)}) collective-permute-start(bf16[2,512,512]{2,1,0:T(8,128)(2,1)} %pad_maximum_fusion.1), channel_id=1, source_target_pairs={{0,2},{2,4},{4,6},{6,8},{8,10},{10,12},{12,14},{14,16},{16,18},{18... | collective-permute-start | bytes 3145736 | tf_op jit(solution)/shard_map/ppermute | solution.py:22
  31.9 103.8 %collective-permute-start.3 = (bf16[2,512,512]{2,1,0:T(8,128)(2,1)}, bf16[2,512,512]{2,1,0:T(8,128)(2,1)}, u32[]{:S(2)}, u32[]{:S(2)}) collective-permute-start(bf16[2,512,512]{2,1,0:T(8,128)(2,1)} %pad_maximum_fusion), channel_id=1, source_target_pairs={{0,4},{2,6},{4,8},{6,10},{8,12},{10,14},{12,16},{14,18},{16,20},{1... | collective-permute-start | bytes 3145736 | tf_op jit(solution)/shard_map/ppermute | solution.py:22
  37.3 57.0 %copy-start.7 = (f32[128]{0:T(128)S(1)}, f32[128]{0:T(128)}, u32[]{:S(2)}) copy-start(f32[128]{0:T(128)} %param.18) | copy-start | bytes 1540
  37.3 57.0 %copy-start.8 = (f32[128]{0:T(128)S(1)}, f32[128]{0:T(128)}, u32[]{:S(2)}) copy-start(f32[128]{0:T(128)} %param.19) | copy-start | bytes 1540
  38.7 97.0 %collective-permute-start.2 = (bf16[2,512,512]{2,1,0:T(8,128)(2,1)}, bf16[2,512,512]{2,1,0:T(8,128)(2,1)S(1)}, u32[]{:S(2)}, u32[]{:S(2)}) collective-permute-start(bf16[2,512,512]{2,1,0:T(8,128)(2,1)} %pad_maximum_fusion), channel_id=1, source_target_pairs={{0,2},{2,4},{4,6},{6,8},{8,10},{10,12},{12,14},{14,16},{16,18},{18... | collective-permute-start | bytes 3145736 | tf_op jit(solution)/shard_map/ppermute | solution.py:22
  94.3 1.1 copy-start.1
  95.4 0.9 copy-start.6
  131.7 1.0 copy-start.2
  132.7 1.0 copy-start.4
  135.7 45.5 %collective-permute-start.10 = (bf16[4,2,2,2,8,768]{5,4,0,1,2,3:T(8,128)(2,1)}, bf16[4,2,2,2,8,768]{5,4,0,1,2,3:T(8,128)(2,1)}, u32[]{:S(2)}, u32[]{:S(2)}) collective-permute-start(bf16[4,2,2,2,8,768]{5,4,0,1,2,3:T(8,128)(2,1)} %fusion.1), channel_id=1, source_target_pairs={{0,2},{2,0},{4,6},{6,4},{8,10},{10,8},{12,14},{14,12},{16,18},{18,... | collective-permute-start | bytes 1179656 | tf_op jit(solution)/shard_map/ppermute | solution.py:254
  171.4 1.0 copy-start.3
  172.4 1.0 copy-start.5
  174.6 11.1 %collective-permute-start.14 = (bf16[4,2,2,2,8,768]{5,4,3,2,1,0:T(8,128)(2,1)S(1)}, bf16[4,2,2,2,8,768]{5,4,3,2,1,0:T(8,128)(2,1)S(1)}, u32[]{:S(2)}, u32[]{:S(2)}) collective-permute-start(bf16[4,2,2,2,8,768]{5,4,3,2,1,0:T(8,128)(2,1)S(1)} %fusion), channel_id=1, source_target_pairs={{0,4},{2,6},{4,0},{6,2},{8,12},{10,14},{12,8},{14,10},{16,20},{18,... | collective-permute-start | bytes 1179656 | tf_op jit(solution)/shard_map/ppermute | solution.py:254
  177.1 12.8 %copy-start.12 = (f32[4,128,768]{2,1,0:T(8,128)S(1)}, f32[4,128,768]{2,1,0:T(8,128)}, u32[]{:S(2)}) copy-start(f32[4,128,768]{2,1,0:T(8,128)} %get-tuple-element.26) | copy-start | bytes 4718596
  177.1 134.9 %collective-permute-start.6 = (bf16[2,512,512]{2,1,0:T(8,128)(2,1)}, bf16[2,512,512]{2,1,0:T(8,128)(2,1)S(1)}, u32[]{:S(2)}, u32[]{:S(2)}) collective-permute-start(bf16[2,512,512]{2,1,0:T(8,128)(2,1)} %copy-done.4), channel_id=1, source_target_pairs={{2,0},{4,2},{6,4},{8,6},{10,8},{12,10},{14,12},{16,14},{18,16},{20... | collective-permute-start | bytes 3145736 | tf_op jit(solution)/shard_map/ppermute | solution.py:22
  178.5 133.5 %collective-permute-start.7 = (bf16[2,512,512]{2,1,0:T(8,128)(2,1)}, bf16[2,512,512]{2,1,0:T(8,128)(2,1)S(1)}, u32[]{:S(2)}, u32[]{:S(2)}) collective-permute-start(bf16[2,512,512]{2,1,0:T(8,128)(2,1)} %copy-done.2), channel_id=1, source_target_pairs={{4,0},{6,2},{8,4},{10,6},{12,8},{14,10},{16,12},{18,14},{20,16},{2... | collective-permute-start | bytes 3145736 | tf_op jit(solution)/shard_map/ppermute | solution.py:22
  179.8 132.7 %collective-permute-start.8 = (bf16[2,512,512]{2,1,0:T(8,128)(2,1)}, bf16[2,512,512]{2,1,0:T(8,128)(2,1)S(1)}, u32[]{:S(2)}, u32[]{:S(2)}) collective-permute-start(bf16[2,512,512]{2,1,0:T(8,128)(2,1)} %copy-done.5), channel_id=1, source_target_pairs={{2,0},{4,2},{6,4},{8,6},{10,8},{12,10},{14,12},{16,14},{18,16},{20... | collective-permute-start | bytes 3145736 | tf_op jit(solution)/shard_map/ppermute | solution.py:22
  181.1 131.4 %collective-permute-start.9 = (bf16[2,512,512]{2,1,0:T(8,128)(2,1)}, bf16[2,512,512]{2,1,0:T(8,128)(2,1)S(1)}, u32[]{:S(2)}, u32[]{:S(2)}) collective-permute-start(bf16[2,512,512]{2,1,0:T(8,128)(2,1)} %copy-done.3), channel_id=1, source_target_pairs={{4,0},{6,2},{8,4},{10,6},{12,8},{14,10},{16,12},{18,14},{20,16},{2... | collective-permute-start | bytes 3145736 | tf_op jit(solution)/shard_map/ppermute | solution.py:22
  185.7 47.6 %collective-permute-start.11 = (bf16[4,2,2,8,768]{4,3,0,1,2:T(8,128)(2,1)S(1)}, bf16[4,2,2,8,768]{4,3,0,1,2:T(8,128)(2,1)S(1)}, u32[]{:S(2)}, u32[]{:S(2)}) collective-permute-start(bf16[4,2,2,8,768]{4,3,0,1,2:T(8,128)(2,1)S(1)} %fusion.3), channel_id=1, source_target_pairs={{0,4},{2,6},{4,0},{6,2},{8,12},{10,14},{12,8},{14,10},{16,20},{18,... | collective-permute-start | bytes 589832 | tf_op jit(solution)/shard_map/ppermute | solution.py:254
  190.0 122.0 %copy-start.10 = (f32[2,512,512]{2,1,0:T(8,128)S(1)}, f32[2,512,512]{2,1,0:T(8,128)}, u32[]{:S(2)}) copy-start(f32[2,512,512]{2,1,0:T(8,128)} %get-tuple-element.19) | copy-start | bytes 6291460
  233.2 53.6 %collective-permute-start.15 = (bf16[4,2,2,8,768]{4,3,2,1,0:T(8,128)(2,1)S(1)}, bf16[4,2,2,8,768]{4,3,2,1,0:T(8,128)(2,1)S(1)}, u32[]{:S(2)}, u32[]{:S(2)}) collective-permute-start(bf16[4,2,2,8,768]{4,3,2,1,0:T(8,128)(2,1)S(1)} %fusion.4), channel_id=1, source_target_pairs={{0,2},{2,0},{4,6},{6,4},{8,10},{10,8},{12,14},{14,12},{16,18},{18,... | collective-permute-start | bytes 589832 | tf_op jit(solution)/shard_map/ppermute | solution.py:254
  286.8 8.7 %collective-permute-start.12 = (bf16[4,2,8,768]{3,2,0,1:T(8,128)(2,1)S(1)}, bf16[4,2,8,768]{3,2,0,1:T(8,128)(2,1)S(1)}, u32[]{:S(2)}, u32[]{:S(2)}) collective-permute-start(bf16[4,2,8,768]{3,2,0,1:T(8,128)(2,1)S(1)} %fusion.5), channel_id=1, source_target_pairs={{0,8},{2,10},{4,12},{6,14},{8,0},{10,2},{12,4},{14,6},{16,24},{18,... | collective-permute-start | bytes 294920 | tf_op jit(solution)/shard_map/ppermute | solution.py:254
  295.6 5.1 %collective-permute-start.16 = (bf16[4,2,8,768]{3,2,1,0:T(8,128)(2,1)S(1)}, bf16[4,2,8,768]{3,2,1,0:T(8,128)(2,1)S(1)}, u32[]{:S(2)}, u32[]{:S(2)}) collective-permute-start(bf16[4,2,8,768]{3,2,1,0:T(8,128)(2,1)S(1)} %fusion.6), channel_id=1, source_target_pairs={{0,8},{2,10},{4,12},{6,14},{8,0},{10,2},{12,4},{14,6},{16,24},{18,... | collective-permute-start | bytes 294920 | tf_op jit(solution)/shard_map/ppermute | solution.py:254
  300.7 5.0 %collective-permute-start.13 = (bf16[4,8,768]{2,1,0:T(8,128)(2,1)S(1)}, bf16[4,8,768]{2,1,0:T(8,128)(2,1)S(1)}, u32[]{:S(2)}, u32[]{:S(2)}) collective-permute-start(bf16[4,8,768]{2,1,0:T(8,128)(2,1)S(1)} %fusion.8), channel_id=1, source_target_pairs={{0,16},{2,18},{4,20},{6,22},{8,24},{10,26},{12,28},{14,30},{16,0},... | collective-permute-start | bytes 147464 | tf_op jit(solution)/shard_map/ppermute | solution.py:254
  305.7 5.0 %collective-permute-start.17 = (bf16[4,8,768]{2,1,0:T(8,128)(2,1)S(1)}, bf16[4,8,768]{2,1,0:T(8,128)(2,1)S(1)}, u32[]{:S(2)}, u32[]{:S(2)}) collective-permute-start(bf16[4,8,768]{2,1,0:T(8,128)(2,1)S(1)} %fusion.9), channel_id=1, source_target_pairs={{0,16},{2,18},{4,20},{6,22},{8,24},{10,26},{12,28},{14,30},{16,0},... | collective-permute-start | bytes 147464 | tf_op jit(solution)/shard_map/ppermute | solution.py:254
  312.5 1.6 copy-start.11

commit v2 on v1

v2 whole, which is shorter than its diff:
```python
import functools
import math

import jax
import jax.numpy as jnp
from jax import lax
from jax.experimental import pallas as pl
from jax.experimental.pallas import tpu as pltpu
from jax.sharding import PartitionSpec as P

WINDOW = 1024
SCALE = 168.0 ** (-0.5)
EPSILON = 1e-06
ROPE_BASE = 10000.0
NT = (((1,), (1,)), ((), ()))
MESH = pl.DeviceIdType.MESH


def remote(src, dst, send_sem, recv_sem, target):
    return pltpu.make_async_remote_copy(
        src_ref=src, dst_ref=dst, send_sem=send_sem, recv_sem=recv_sem,
        device_id={"seq": target}, device_id_type=MESH,
    )


def dot(a, b):
    return jnp.dot(a, b, preferred_element_type=jnp.float32)


def dot_nt(a, b):
    return lax.dot_general(a, b, NT, preferred_element_type=jnp.float32)


def swap_halves(x):
    return pltpu.roll(x, x.shape[-1] // 2, 1)


def norm_parts(raw):
    rstd = lax.rsqrt(jnp.mean(raw * raw, axis=-1, keepdims=True) + EPSILON)
    return raw * rstd, rstd


def rotate(normed, cos, sin):
    return normed * cos + swap_halves(normed) * sin


def prepare_back(grad, unit, rstd, gain, cos, sin):
    inner = (grad * cos + swap_halves(grad * sin)) * gain
    return rstd * (inner - unit * jnp.mean(inner * unit, axis=-1, keepdims=True))


def attention_kernel(
    count, packed, cos, sin, q_gain, k_gain, x_own, dy_t, q, d_out, k_all, v_all, k_own, v_own,
    query_out, key_out, value_out, *rest
):
    sketch_outs = rest[: 4 if packed else 1]
    rest = rest[len(sketch_outs) :]
    (k_s, v_s, kt_s, vt_s, dk_s, dv_s, e_s, dp_s, p_s, ds_s, sk_s, halo_land, ret_send, ret_land,
     own_s, x_land, halo_ss, halo_rs, ret_ss, ret_rs, x_ss, x_rs) = rest[:22]
    if packed:
        sk_send, sk_land, sk_ss, sk_rs = rest[22:]
    tok = q.shape[0]
    hd = q_gain.shape[1]
    group = q.shape[1] // hd
    sub = tok // 2
    span = 3 * tok
    band = 5 * sub
    cols = group * sub
    exponent = SCALE * math.log2(math.e)
    g = pl.program_id(0)
    heads = k_all.shape[1] // hd
    me = lax.axis_index("seq")

    def halo_copy(dist, kind, head):
        src = (k_all, v_all)[kind].at[:, pl.ds(pl.multiple_of(head * hd, hd), hd)]
        return remote(src, halo_land.at[dist - 1, kind, head], halo_ss.at[dist - 1, kind, head],
                      halo_rs.at[dist - 1, kind, head], lax.rem(me + dist, count))

    def x_copy(dist):
        return remote(x_own, x_land.at[dist - 1], x_ss.at[dist - 1], x_rs.at[dist - 1],
                      lax.rem(me + dist, count))

    def ret_copy(dist, head):
        return remote(ret_send.at[dist - 1, head], ret_land.at[dist - 1, head],
                      ret_ss.at[dist - 1, head], ret_rs.at[dist - 1, head],
                      lax.rem(me - dist + count, count))

    def sketch_copy(step, head):
        to = lax.rem(me + step, count)
        return remote(sk_send.at[head, to], sk_land.at[head, me], sk_ss.at[head, step],
                      sk_rs.at[head, step], to)

    @pl.when(g == 0)
    def _():
        barrier = pltpu.get_barrier_semaphore()

        @pl.loop(1, count)
        def _(step):
            pl.semaphore_signal(barrier, inc=1, device_id={"seq": lax.rem(me + step, count)},
                                device_id_type=MESH)

        pl.semaphore_wait(barrier, count - 1)
        for dist in (1, 2):
            @pl.when(me + dist < count)
            def _():
                x_copy(dist).start()

        @pl.loop(0, heads)
        def _(head):
            for dist in (1, 2):
                @pl.when(me + dist < count)
                def _():
                    halo_copy(dist, 0, head).start()
                    halo_copy(dist, 1, head).start()

        for dist in (1, 2):
            @pl.when(me < dist)
            def _():
                halo_land[dist - 1] = jnp.zeros(halo_land.shape[1:], jnp.bfloat16)
                x_land[dist - 1] = jnp.zeros(x_land.shape[1:], jnp.bfloat16)

            @pl.when(me + dist >= count)
            def _():
                ret_land[dist - 1] = jnp.zeros(ret_land.shape[1:], jnp.bfloat16)

    for dist in (1, 2):
        @pl.when(me >= dist)
        def _():
            halo_copy(dist, 0, g).wait_recv()
            halo_copy(dist, 1, g).wait_recv()

    valid = (jnp.where(me >= 1, 1.0, 0.0), jnp.where(me >= 2, 1.0, 0.0))
    near = (halo_land.at[0, 0, g], halo_land.at[0, 1, g])
    far = (halo_land.at[1, 0, g], halo_land.at[1, 1, g])

    for part, raw, val in ((0, far[0], far[1]), (1, near[0], near[1]), (2, k_own, v_own)):
        rows = pl.ds(part * tok, tok)
        unit, _ = norm_parts(raw[...].astype(jnp.float32))
        prep = rotate(unit * k_gain[...], cos[rows, :], sin[rows, :])
        k_s[rows, :] = prep.astype(jnp.bfloat16)
        kt_s[:, part * tok : (part + 1) * tok] = prep.T.astype(jnp.bfloat16)
        v_s[rows, :] = val[...]
        vt_s[:, part * tok : (part + 1) * tok] = val[...].astype(jnp.float32).T.astype(jnp.bfloat16)

    key_at = lax.broadcasted_iota(jnp.int32, (sub, cols), 0)
    query_at = lax.broadcasted_iota(jnp.int32, (sub, cols), 1) % sub
    older = key_at > query_at
    weight = jnp.where(older, valid[1], 1.0)

    for i in range(2):
        rows = slice(i * sub, (i + 1) * sub)
        own_rows = pl.ds(2 * tok + i * sub, sub)
        q_cos, q_sin = cos[own_rows, :], sin[own_rows, :]
        units = []
        preps = []
        for h in range(group):
            unit, rstd = norm_parts(q[rows, h * hd : (h + 1) * hd].astype(jnp.float32))
            units.append((unit, rstd))
            preps.append(rotate(unit * q_gain[...], q_cos, q_sin).astype(jnp.bfloat16))
        query = jnp.concatenate(preps, axis=0)
        grad = jnp.concatenate([d_out[rows, h * hd : (h + 1) * hd] for h in range(group)], axis=0)

        total = jnp.zeros((1, cols), jnp.float32)
        mixed = jnp.zeros((1, cols), jnp.float32)
        for t in range(4):
            at = slice((i + t) * sub, (i + t + 1) * sub)
            score = dot_nt(k_s[at, :], query)
            grad_p = dot_nt(v_s[at, :], grad)
            if t == 0:
                last = slice((i + 4) * sub, (i + 5) * sub)
                score = jnp.where(older, score, dot_nt(k_s[last, :], query))
                grad_p = jnp.where(older, grad_p, dot_nt(v_s[last, :], grad))
            e = jnp.exp2(score * exponent)
            here = slice(t * sub, (t + 1) * sub)
            e_s[i, here, :] = e
            dp_s[i, here, :] = grad_p
            mixed = mixed + jnp.sum(e * grad_p, axis=0, keepdims=True)
            if t == 0:
                total = total + jnp.sum(e * weight, axis=0, keepdims=True)
            else:
                part = jnp.sum(e, axis=0, keepdims=True)
                shard = (i + t) // 2
                total = total + (part if shard == 2 else part * valid[1 - shard])
        inverse = 1.0 / total
        delta = mixed * inverse
        for t in range(4):
            here = slice(t * sub, (t + 1) * sub)
            prob = e_s[i, here, :] * inverse
            ds = prob * (dp_s[i, here, :] - delta)
            if t == 0:
                last = slice(4 * sub, 5 * sub)
                p_s[i, here, :] = jnp.where(older, prob, 0.0).astype(jnp.bfloat16)
                p_s[i, last, :] = jnp.where(older, 0.0, prob).astype(jnp.bfloat16)
                ds_s[i, here, :] = jnp.where(older, ds, 0.0).astype(jnp.bfloat16)
                ds_s[i, last, :] = jnp.where(older, 0.0, ds).astype(jnp.bfloat16)
            else:
                p_s[i, here, :] = prob.astype(jnp.bfloat16)
                ds_s[i, here, :] = ds.astype(jnp.bfloat16)

        keys = slice(i * sub, i * sub + band)
        dv = dot(p_s[i], grad)
        dk = dot(ds_s[i], query)
        if i == 0:
            dv_s[:band, :] = dv
            dk_s[:band, :] = dk
            dv_s[band:, :] = jnp.zeros((span - band, hd), jnp.float32)
            dk_s[band:, :] = jnp.zeros((span - band, hd), jnp.float32)
        else:
            dv_s[keys, :] += dv
            dk_s[keys, :] += dk
        attn_t = dot(vt_s[:, keys], p_s[i]).astype(jnp.bfloat16)
        dq = dot(kt_s[:, keys], ds_s[i]).T * SCALE
        for h in range(group):
            unit, rstd = units[h]
            part = prepare_back(
                dq[h * sub : (h + 1) * sub, :], unit, rstd, q_gain[...], q_cos, q_sin
            ).astype(jnp.bfloat16)
            query_out[rows, h * hd : (h + 1) * hd] = part
            sk_q = dot(x_own[:, rows], part)
            sk_o = dot_nt(dy_t[:, rows], attn_t[:, h * sub : (h + 1) * sub])
            to_q = slice(h * hd, (h + 1) * hd)
            to_o = slice((group + 2 + h) * hd, (group + 3 + h) * hd)
            if i == 0:
                sk_s[:, to_q] = sk_q
                sk_s[:, to_o] = sk_o
            else:
                sk_s[:, to_q] += sk_q
                sk_s[:, to_o] += sk_o

    @pl.when(g == 0)
    def _():
        for dist in (1, 2):
            @pl.when(me >= dist)
            def _():
                x_copy(dist).wait_recv()

    sk_k = jnp.zeros((x_own.shape[0], hd), jnp.float32)
    sk_v = jnp.zeros((x_own.shape[0], hd), jnp.float32)
    for part, raw, out in ((0, far[0], ret_send.at[1, g]), (1, near[0], ret_send.at[0, g]),
                           (2, k_own, own_s.at[g])):
        rows = pl.ds(part * tok, tok)
        unit, rstd = norm_parts(raw[...].astype(jnp.float32))
        dk = prepare_back(
            dk_s[rows, :] * SCALE, unit, rstd, k_gain[...], cos[rows, :], sin[rows, :]
        )
        dv = dv_s[rows, :]
        out[0] = dk.astype(out.dtype)
        out[1] = dv.astype(out.dtype)
        xs = x_own[...] if part == 2 else x_land[1 - part]
        sk_k = sk_k + dot(xs, dk.astype(jnp.bfloat16))
        sk_v = sk_v + dot(xs, dv.astype(jnp.bfloat16))
    for dist in (2, 1):
        @pl.when(me >= dist)
        def _():
            ret_copy(dist, g).start()
    sk_s[:, group * hd : (group + 1) * hd] = sk_k
    sk_s[:, (group + 1) * hd : (group + 2) * hd] = sk_v

    width = sk_s.shape[1]
    if packed:
        mid = width // 2
        parts = sk_s[...].reshape(count, 8, width)
        sk_send[g] = jnp.concatenate([parts[:, :, :mid], parts[:, :, mid:]], axis=1).astype(
            jnp.bfloat16)
        sk_land[g, me] = sk_send[g, me]

        @pl.loop(1, count)
        def _(step):
            sketch_copy(step, g).start()
    else:
        sketch_outs[0][0] = sk_s[...]

    @pl.when(g == heads - 1)
    def _():
        @pl.loop(0, heads)
        def _(head):
            for dist in (1, 2):
                @pl.when(me + dist < count)
                def _():
                    halo_copy(dist, 0, head).wait_send()
                    halo_copy(dist, 1, head).wait_send()
                    ret_copy(dist, head).wait_recv()

                @pl.when(me >= dist)
                def _():
                    ret_copy(dist, head).wait_send()

        for dist in (1, 2):
            @pl.when(me + dist < count)
            def _():
                x_copy(dist).wait_send()

        for h in range(heads):
            at = slice(h * hd, (h + 1) * hd)
            for kind, out in ((0, key_out), (1, value_out)):
                out[:, at] = (own_s[h, kind] + ret_land[0, h, kind].astype(jnp.float32)
                              + ret_land[1, h, kind].astype(jnp.float32)).astype(jnp.bfloat16)

        if packed:
            @pl.loop(0, heads)
            def _(head):
                @pl.loop(1, count)
                def _(step):
                    sketch_copy(step, head).wait()

            mid = width // 2
            wide = group * hd
            for h in range(heads):
                both = jnp.sum(sk_land[h].astype(jnp.float32), axis=0)
                row = jnp.concatenate([both[:8], both[8:]], axis=1)
                sketch_outs[0][:, h * wide : (h + 1) * wide] = row[:, :wide]
                sketch_outs[1][:, h * hd : (h + 1) * hd] = row[:, wide : wide + hd]
                sketch_outs[2][:, h * hd : (h + 1) * hd] = row[:, wide + hd : wide + 2 * hd]
                sketch_outs[3][:, h * wide : (h + 1) * wide] = row[:, wide + 2 * hd :]


def attention(count, cos, sin, q_gain, k_gain, x_t, dy_t, q_raw, d_out, k_raw, values):
    tok, q_cols = q_raw.shape
    kv_cols = k_raw.shape[1]
    hd = q_gain.shape[1]
    heads = kv_cols // hd
    group = q_cols // kv_cols
    rank = x_t.shape[0]
    packed = rank == 8 * count
    wide = group * hd
    width = 2 * wide + 2 * hd
    span, sub = 3 * tok, tok // 2
    cols = group * sub
    bf16, f32 = jnp.bfloat16, jnp.float32
    whole = lambda *shape: pl.BlockSpec(shape, lambda g: (0,) * len(shape))
    q_spec = pl.BlockSpec((tok, wide), lambda g: (0, g))
    k_spec = pl.BlockSpec((tok, hd), lambda g: (0, g))
    hbm = pl.BlockSpec(memory_space=pl.ANY)
    out_specs = [q_spec, whole(tok, kv_cols), whole(tok, kv_cols)]
    out_shape = [
        jax.ShapeDtypeStruct(q_raw.shape, bf16),
        jax.ShapeDtypeStruct(k_raw.shape, bf16),
        jax.ShapeDtypeStruct(k_raw.shape, bf16),
    ]
    scratch = [
        pltpu.VMEM((span, hd), bf16),
        pltpu.VMEM((span, hd), bf16),
        pltpu.VMEM((hd, span), bf16),
        pltpu.VMEM((hd, span), bf16),
        pltpu.VMEM((span, hd), f32),
        pltpu.VMEM((span, hd), f32),
        pltpu.VMEM((2, 4 * sub, cols), f32),
        pltpu.VMEM((2, 4 * sub, cols), f32),
        pltpu.VMEM((2, 5 * sub, cols), bf16),
        pltpu.VMEM((2, 5 * sub, cols), bf16),
        pltpu.VMEM((rank, width), f32),
        pltpu.VMEM((2, 2, heads, tok, hd), bf16),
        pltpu.VMEM((2, heads, 2, tok, hd), bf16),
        pltpu.VMEM((2, heads, 2, tok, hd), bf16),
        pltpu.VMEM((heads, 2, tok, hd), f32),
        pltpu.VMEM((2, rank, tok), bf16),
        pltpu.SemaphoreType.DMA((2, 2, heads)),
        pltpu.SemaphoreType.DMA((2, 2, heads)),
        pltpu.SemaphoreType.DMA((2, heads)),
        pltpu.SemaphoreType.DMA((2, heads)),
        pltpu.SemaphoreType.DMA((2,)),
        pltpu.SemaphoreType.DMA((2,)),
    ]
    if packed:
        for n in (wide, hd, hd, wide):
            out_specs.append(whole(8, heads * n))
            out_shape.append(jax.ShapeDtypeStruct((8, heads * n), f32))
        scratch += [
            pltpu.VMEM((heads, count, 16, width // 2), bf16),
            pltpu.VMEM((heads, count, 16, width // 2), bf16),
            pltpu.SemaphoreType.DMA((heads, count)),
            pltpu.SemaphoreType.DMA((heads, count)),
        ]
    else:
        out_specs.append(pl.BlockSpec((1, rank, width), lambda g: (g, 0, 0)))
        out_shape.append(jax.ShapeDtypeStruct((heads, rank, width), f32))
    return pl.pallas_call(
        functools.partial(attention_kernel, count, packed),
        grid=(heads,),
        in_specs=[whole(span, hd), whole(span, hd), whole(1, hd), whole(1, hd),
                  whole(rank, tok), whole(rank, tok), q_spec, q_spec, hbm, hbm, k_spec, k_spec],
        out_specs=out_specs,
        out_shape=out_shape,
        scratch_shapes=scratch,
        compiler_params=pltpu.CompilerParams(
            dimension_semantics=("arbitrary",), vmem_limit_bytes=56 * 1024 * 1024,
            collective_id=0, has_side_effects=True,
        ),
        cost_estimate=pl.CostEstimate(
            flops=heads * 20 * 5 * sub * tok * group * hd,
            bytes_accessed=heads * 4 * tok * hd * 20,
            transcendentals=heads * 4 * sub * tok * group,
        ),
    )(cos, sin, q_gain, k_gain, x_t, dy_t, q_raw, d_out, k_raw, values, k_raw, values)


def scatter_sum(part, order):
    count = lax.axis_size("seq")
    bits = len(order)
    heads, rank, cols = part.shape
    me = lax.axis_index("seq")
    cur = part.reshape((heads,) + (2,) * bits + (rank // count, cols))
    axes = list(range(bits - 1, -1, -1))
    for bit in order:
        axis = 1 + axes.index(bit)
        axes.remove(bit)
        mine = (me >> bit) & 1
        keep = lax.dynamic_index_in_dim(cur, mine, axis, keepdims=False)
        away = lax.dynamic_index_in_dim(cur, 1 - mine, axis, keepdims=False)
        pairs = [(i, i ^ (1 << bit)) for i in range(count)]
        cur = keep + lax.ppermute(away.astype(jnp.bfloat16), "seq", pairs).astype(jnp.float32)
    return cur


def per_device(
    layer_input, omega_in, upstream, omega_out, q_raw, k_raw, values, d_out, q_gain, k_gain
):
    tok = q_raw.shape[0]
    hd = q_gain.shape[0]
    kv_cols = k_raw.shape[1]
    heads_kv = kv_cols // hd
    group = q_raw.shape[1] // kv_cols
    me = lax.axis_index("seq")
    count = lax.axis_size("seq")

    partial_x = dot(layer_input, omega_in)
    partial_y = dot(upstream, omega_out)
    summed_x, summed_y = lax.psum((partial_x, partial_y), "head")
    x_t = summed_x.astype(jnp.bfloat16).T
    dy_t = summed_y.astype(jnp.bfloat16).T

    half = hd // 2
    inverse_freq = ROPE_BASE ** (-(jnp.arange(half, dtype=jnp.float32) * 2.0 / hd))
    positions = (me - 2) * tok + jnp.arange(3 * tok, dtype=jnp.int32)
    angles = positions.astype(jnp.float32)[:, None] * inverse_freq[None, :]
    cos, sin = jnp.cos(angles), jnp.sin(angles)
    cos = jnp.concatenate([cos, cos], axis=1)
    sin = jnp.concatenate([-sin, sin], axis=1)
    results = attention(
        count, cos, sin, q_gain[None, :], k_gain[None, :], x_t, dy_t, q_raw, d_out, k_raw, values
    )
    if len(results) == 7:
        return tuple(results)
    query_grad, key_grad, value_grad, sketch = results
    all_sketch = scatter_sum(sketch, list(range(count.bit_length() - 1)))

    def columns(first, width):
        piece = all_sketch[:, :, first : first + width]
        return piece.transpose(1, 0, 2).reshape(piece.shape[1], heads_kv * width)

    wide = group * hd
    return (
        query_grad, key_grad, value_grad,
        columns(0, wide), columns(wide, hd), columns(wide + hd, hd), columns(wide + 2 * hd, wide),
    )


def solution(mesh):
    split = P("seq", "head")
    by_head = P("head", None)
    in_specs = (split, by_head, split, by_head, split, split, split, split, P(), P())
    return jax.shard_map(
        per_device, mesh=mesh, in_specs=in_specs, out_specs=(split,) * 7, check_vma=False
    )
```

time: 318 us -> 220 us (0.69)
  Pallas kernels: 71.2 us -> 194 us
  waiting for transfers between devices: 118 us -> 0 us
  starting transfers between devices: 90.6 us -> 0 us
  other arithmetic: 13.4 us -> 4.44 us
  local copies, waits for them, and re-layouts: 14.3 us -> 9.49 us
    pallas_call x2 -> x1, Pallas kernels: 71.2 us -> 194 us  [attention(): pl.pallas_call(functools.partial(attention_kernel, count, packed), grid=(...]
    ppermute x18 -> x0, waiting for transfers between devices: 118 us -> none  [the longest x8 66.7 us: scatter_sum(): lax.ppermute(away.astype(jnp.bfloat16), 'seq', pairs).astype(jnp.float32)]
    ppermute x18 -> x0, starting transfers between devices: 90.6 us -> none  [the longest x8 62.3 us: scatter_sum(): lax.ppermute(away.astype(jnp.bfloat16), 'seq', pairs).astype(jnp.float32)]
    concatenate x4 -> x0, other arithmetic: 3.97 us -> none  [the longest x1 1.13 us: per_device(): value_grad = jnp.concatenate([s[1] for s in sums], axis=1)]
    convert_element_type x8 -> x0, local copies, waits for them, and re-layouts: 3.25 us -> none  [scatter_sum(): away.astype(jnp.bfloat16)]
    unnamed x28 -> x25, local copies, waits for them, and re-layouts: 9.23 us -> 9.49 us
  transfers between devices with their start and end apart: 18 -> 0, of which waited for: 8 -> 0; matrix products, arithmetic and copies ran while one was open for 5% -> 0% of each run, Pallas kernels for 22% -> 0%
where the time goes in v2:
time: 220 us; the launch traced here: 218 us
  Pallas kernels  194 us (88%)
  local copies, waits for them, and re-layouts  9.49 us (4%)
  blocking collectives  5.63 us (3%)
  other arithmetic  4.44 us (2%)
  matrix products  3.24 us (1%)
    pallas_call x1, Pallas kernels, attention(): pl.pallas_call(functools.partial(attention_kernel, count, packed), grid=(...  194 us
    unnamed x25, local copies, waits for them, and re-layouts  9.49 us
    psum x1, blocking collectives, per_device(): summed_x, summed_y = lax.psum((partial_x, partial_y), 'head')  5.63 us

profile of v2, /device:TPU:0, one launch (start us, length us, event | category | flops | bytes accessed | tf_op | source)
XLA Modules:
  0.0 217.9 jit_solution(8295747542829865694)
XLA Ops:
  0.6 0.0 copy-start
  0.7 0.0 copy-start.1
  0.7 0.0 copy-start.4
  0.7 1.7 copy-done
  2.4 2.2 %fusion.1 = f32[512,128]{0,1:T(8,128)S(1)} fusion(bf16[512,2688]{1,0:T(8,128)(2,1)S(1)} %copy-done, bf16[2688,128]{1,0:T(8,128)(2,1)} %param.11), kind=kOutput, calls=%fused_computation.9 | convolution fusion | flops 352321536 | bytes 3702784 | tf_op jit(solution)/shard_map/dot_general | solution.py:27
  4.6 0.0 copy-done.1
  4.6 0.0 copy-done.4
  4.6 1.0 fusion.2
  5.7 5.6 %all-reduce.2 = (bf16[512,128]{0,1:T(8,128)(2,1)}, bf16[512,128]{0,1:T(8,128)(2,1)}) all-reduce(f32[512,128]{0,1:T(8,128)S(1)} %fusion.1, f32[512,128]{0,1:T(8,128)S(1)} %fusion.2), channel_id=1, replica_groups=mesh['seq'=16,'head'=2] {'head'}, use_global_device_ids=true, to_apply=%region_0.0 | all-reduce | flops 131072 | bytes 786432 | tf_op jit(solution)/shard_map/psum | solution.py:428
  11.3 2.8 %fusion = (f32[1536,64]{1,0:T(8,128)S(1)}, f32[1536,64]{1,0:T(8,128)S(1)}, f32[1536,64]{1,0:T(8,128)S(1)}) fusion(f32[64]{0:T(128)S(1)} %negate_power_fusion, f32[1536]{0:T(1024)S(1)} %add_convert_fusion), kind=kLoop, calls=%fused_computation.4 | loop fusion | flops 196608 | bytes 1186048 | tf_op jit(solution)/shard_map/neg | solution.py:438
  14.1 1.6 pad_maximum_fusion
  15.7 194.3 %shard_map.153 = (bf16[512,2048]{1,0:T(8,128)(2,1)}, bf16[512,1024]{1,0:T(8,128)(2,1)}, bf16[512,1024]{1,0:T(8,128)(2,1)}, f32[8,2048]{1,0:T(8,128)}, f32[8,1024...) custom-call(f32[1536,128]{1,0:T(8,128)} %get-tuple-element.12.cos, f32[1536,128]{1,0:T(8,128)} %get-tuple-element.13.sin, ...), custom_call_target="tpu_custom_call" | custom-call | flops 26843545600 | bytes 41943040 | tf_op jit(solution)/shard_map/pallas_call | solution.py:377
  210.1 0.0 copy-start.3
  210.1 0.0 copy-start.2
  210.1 3.3 %copy.32 = bf16[512,2048]{1,0:T(8,128)(2,1)} copy(bf16[512,2048]{1,0:T(8,128)(2,1)} %get-tuple-element.21) | data formatting | bytes 4194304
  213.4 0.0 copy-done.3
  213.4 0.0 copy-start.6
  213.4 0.0 copy-start.8
  213.4 0.0 copy-start.7
  213.4 0.0 copy-start.5
  213.4 1.0 copy.33
  214.4 0.0 copy-done.2
  214.4 1.0 copy.34
  215.4 0.0 copy-done.6
  215.4 0.6 copy.35
  216.0 0.0 copy-done.8
  216.0 0.6 copy.36
  216.6 0.0 copy-done.7
  216.6 0.6 copy.37
  217.2 0.0 copy-done.5
  217.2 0.6 copy.38
  (2 shorter events, 0.0 us)
Async XLA Ops:
  0.6 1.8 copy-start
  0.7 4.0 %copy-start.1 = (bf16[512,2688]{1,0:T(8,128)(2,1)S(1)}, bf16[512,2688]{1,0:T(8,128)(2,1)}, u32[]{:S(2)}) copy-start(bf16[512,2688]{1,0:T(8,128)(2,1)} %param.12) | copy-start | bytes 8257540
  0.7 4.0 %copy-start.4 = (bf16[2688,128]{1,0:T(8,128)(2,1)S(1)}, bf16[2688,128]{1,0:T(8,128)(2,1)}, u32[]{:S(2)}) copy-start(bf16[2688,128]{1,0:T(8,128)(2,1)} %param.13) | copy-start | bytes 2064388
  210.1 3.3 %copy-start.3 = (bf16[512,1024]{1,0:T(8,128)(2,1)S(1)}, bf16[512,1024]{1,0:T(8,128)(2,1)}, u32[]{:S(2)}) copy-start(bf16[512,1024]{1,0:T(8,128)(2,1)} %get-tuple-element.22) | copy-start | bytes 3145732
  210.1 4.3 %copy-start.2 = (bf16[512,1024]{1,0:T(8,128)(2,1)S(1)}, bf16[512,1024]{1,0:T(8,128)(2,1)}, u32[]{:S(2)}) copy-start(bf16[512,1024]{1,0:T(8,128)(2,1)} %get-tuple-element.23) | copy-start | bytes 3145732
  213.4 2.0 copy-start.6
  213.4 2.6 %copy-start.8 = (f32[8,1024]{1,0:T(8,128)S(1)}, f32[8,1024]{1,0:T(8,128)}, u32[]{:S(2)}) copy-start(f32[8,1024]{1,0:T(8,128)} %get-tuple-element.25) | copy-start | bytes 98308
  213.4 3.2 %copy-start.7 = (f32[8,1024]{1,0:T(8,128)S(1)}, f32[8,1024]{1,0:T(8,128)}, u32[]{:S(2)}) copy-start(f32[8,1024]{1,0:T(8,128)} %get-tuple-element.26) | copy-start | bytes 98308
  213.4 3.8 %copy-start.5 = (f32[8,2048]{1,0:T(8,128)S(1)}, f32[8,2048]{1,0:T(8,128)}, u32[]{:S(2)}) copy-start(f32[8,2048]{1,0:T(8,128)} %get-tuple-element.27) | copy-start | bytes 196612
